TPU v7x, 128 devices: a whole 4x4x4 slice. The times are simulated.
128 devices in a mesh: expert: 16 (over x, z_lo, core), tensor: 8 (over z_hi, y).
Axes of the slice: x: 4, y: 4, z: 4 (z_hi: 2, z_lo: 2; z = z_hi * 2 + z_lo), core: 2. Of those that a mesh axis runs over, the one named last changes fastest.
Arguments:
- learner_delta: bfloat16 [128, 56, 16, 1024], P(('expert', 'tensor')), may hold values from -3 to 3
- owner_block: int32 [128], replicated, may hold values from 0 to 127, each once
- expert_shadow: float32 [16, 7168, 1024], P('expert', None, 'tensor'), may hold values from -10 to 10, as said below
- tile_mode: int32 [16, 56, 8], P('expert', None, 'tensor'), may hold values from 0 to 1
- attn_delta: bfloat16 [512, 16384], P(('expert', 'tensor')), may hold values from -3 to 3
- attn_shadow: float32 [512, 16384], P(None, 'tensor'), may hold values from -10 to 10, as said below
Outputs:
- expert_new: float32 [16, 7168, 1024], P('expert', None, 'tensor')
- expert_codes: bfloat16 [16, 7168, 1024], P('expert', None, 'tensor')
- expert_amax: float32 [16, 56, 1024], P('expert', None, 'tensor')
- attn_new: float32 [512, 16384], P(None, 'tensor')
- attn_codes: bfloat16 [512, 16384], P(None, 'tensor')
- attn_amax: float32 [4, 128], P(None, 'tensor')
Inputs may be any that keep to these rules, and one draw needn't show every extreme that they name: `owner_block`: each row block number appears once. `expert_shadow`: finite real weights. `attn_shadow`: finite real weights.
All inputs are finite; a program needn't handle non-finite values.
Results may differ from a plain program's by a relative error of at most 0.001.
Values may be sent and summed in bfloat16 or wider, within the bound.
A program may use at most 128 MiB of HBM per device.

v0:
```python
import jax
import jax.numpy as jnp
from jax import lax
from jax.sharding import PartitionSpec as P

BLK = 128


def expert_quantize(updated, tile_mode):
    magnitude = jnp.abs(updated)
    count_lead = updated.shape[0]
    count_rows = updated.shape[1]
    count_cols = updated.shape[2]
    column_max = magnitude.reshape(count_lead, count_rows // BLK, BLK, count_cols).max(axis=2)
    tile_max = column_max.reshape(count_lead, count_rows // BLK, count_cols // BLK, BLK).max(axis=3)
    tile_wide = jnp.repeat(tile_max, BLK, axis=2)
    mode_wide = jnp.repeat(tile_mode, BLK, axis=2)
    chosen = jnp.where(mode_wide == 0, tile_wide, column_max)
    codes = (updated / (jnp.repeat(chosen, BLK, axis=1) + 1e-06)).astype(jnp.bfloat16)
    return (codes, chosen)


def attention_quantize(updated):
    count_rows = updated.shape[0]
    count_cols = updated.shape[1]
    tile_max = (
        jnp.abs(updated).reshape(count_rows // BLK, BLK, count_cols // BLK, BLK).max(axis=(1, 3))
    )
    spread_max = jnp.repeat(jnp.repeat(tile_max, BLK, axis=0), BLK, axis=1)
    codes = (updated / (spread_max + 1e-06)).astype(jnp.bfloat16)
    return (codes, tile_max)


def on_device(learner_delta, owner_block, expert_shadow, tile_mode, attn_delta, attn_shadow):
    expert_count = lax.axis_size("expert")
    tensor_count = lax.axis_size("tensor")
    learner_piece = learner_delta[0]
    block_rows = learner_piece.shape[0]
    column_share = expert_shadow.shape[2]
    outgoing = learner_piece.reshape(block_rows, expert_count * tensor_count, column_share)
    arrived = lax.all_to_all(
        outgoing, ("expert", "tensor"), split_axis=1, concat_axis=0, tiled=True
    )
    received = arrived.reshape(expert_count * tensor_count, block_rows, column_share)
    placed = jnp.zeros_like(received).at[owner_block].set(received)
    full_delta = placed.reshape(1, expert_count * tensor_count * block_rows, column_share)
    expert_new = expert_shadow + full_delta.astype(jnp.float32)
    expert_codes, expert_amax = expert_quantize(expert_new, tile_mode)
    attn_share = attn_shadow.shape[1]
    gathered = lax.all_gather(attn_delta, ("expert", "tensor"), axis=0, tiled=True)
    own_columns = lax.dynamic_slice_in_dim(
        gathered, lax.axis_index("tensor") * attn_share, attn_share, 1
    )
    attn_new = attn_shadow + own_columns.astype(jnp.float32)
    attn_codes, attn_amax = attention_quantize(attn_new)
    return (expert_new, expert_codes, expert_amax, attn_new, attn_codes, attn_amax)


def solution(mesh):
    return jax.shard_map(
        on_device,
        mesh=mesh,
        in_specs=(
            P(("expert", "tensor"), None, None, None),
            P(),
            P("expert", None, "tensor"),
            P("expert", None, "tensor"),
            P(("expert", "tensor"), None),
            P(None, "tensor"),
        ),
        out_specs=(
            P("expert", None, "tensor"),
            P("expert", None, "tensor"),
            P("expert", None, "tensor"),
            P(None, "tensor"),
            P(None, "tensor"),
            P(None, "tensor"),
        ),
        check_vma=False,
    )
```

profile of v0, /device:TPU:1, one launch (start us, length us, event | category | flops | bytes accessed | tf_op | source)
XLA Modules:
  0.0 392.6 jit_solution(5826238129446879556)
XLA Ops:
  7.2 0.7 all-gather.3.cloned.1.call-update
  7.9 2.7 reshape_squeeze.3
  10.6 2.4 copy.14
  13.0 11.5 %all-to-all-start = ((bf16[56,128,128]{2,0,1:T(8,128)(2,1)}), bf16[56,128,128]{2,0,1:T(8,128)(2,1)S(1)}, u32[]{:S(2)}, u32[]{:S(2)}) async-start(bf16[56,128,128]{2,0,1:T(8,128)(2,1)} %copy.14), calls=%async_computation | async-start | bytes 3670016 | tf_op jit(solution)/shard_map/all_to_all | solution.py:41
  24.6 31.2 %all-to-all-done = bf16[56,128,128]{2,0,1:T(8,128)(2,1)S(1)} async-done(((bf16[56,128,128]{2,0,1:T(8,128)(2,1)}), bf16[56,128,128]{2,0,1:T(8,128)(2,1)S(1)}, u32[]{:S(2)}, u32[]{:S(2)}) %all-to-all-start) | async-done | bytes 1835040 | tf_op jit(solution)/shard_map/all_to_all | solution.py:41
  55.8 1.2 copy-done.3
  57.0 0.2 broadcast_in_dim.17
  57.3 11.9 %scatter_fusion = bf16[128,56,128]{2,1,0:T(8,128)(2,1)S(1)} fusion(bf16[128,56,128]{2,1,0:T(8,128)(2,1)S(1)} %broadcast_in_dim.17, s32[128]{0:T(128)S(1)} %compare_select_fusion, bf16[128,56,128]{2,1,0:T(8,128)(2,1)} %bitcast.42), kind=kCustom, calls=%fused_computation | custom fusion | bytes 5505536 | tf_op jit(solution)/shard_map/scatter | solution.py:45
  69.2 3.1 abs_reduce_fusion
  72.3 2.4 abs.6
  74.6 0.7 copy-done
  75.3 2.5 reduce_max.39
  77.8 0.1 bitcast_reduce_fusion.1
  77.9 0.7 bitcast_select_fusion
  78.7 0.2 broadcast_in_dim.19
  78.9 0.9 copy-done.1
  79.9 1.7 fusion.1
  81.6 270.5 %all-gather.3.cloned.1.call-done = bf16[128,4,16384]{2,1,0:T(4,128)(2,1)} async-done(((bf16[1,4,16384]{2,1,0:T(4,128)(2,1)}), bf16[128,4,16384]{2,1,0:T(4,128)(2,1)}) %all-gather.3.cloned.1.call-update) | async-done | bytes 16777232 | tf_op jit(solution)/shard_map/all_gather | solution.py:50
  352.1 23.7 %reshape.156 = bf16[512,16384]{1,0:T(8,128)(2,1)} reshape(bf16[128,4,16384]{2,1,0:T(4,128)(2,1)} %all-gather.3.cloned.1.call-done) | data formatting | bytes 33554432
  375.8 4.4 %abs_bitcast_fusion = (f32[64,8,16,128]{3,1,2,0:T(8,128)S(1)}, f32[512,2048]{1,0:T(8,128)S(1)}) fusion(f32[512,2048]{1,0:T(8,128)} %param.11, bf16[512,16384]{1,0:T(8,128)(2,1)} %reshape.156, s32[]{:T(128)S(6)} %select_n.24), kind=kLoop, calls=%fused_computation.4 | loop fusion | flops 3145728 | bytes 14680068
  380.2 0.9 copy.15
  381.1 0.3 bitcast_reduce_fusion
  381.6 1.1 broadcast_in_dim.21
  382.7 3.0 fusion
  (17 shorter events, 0.2 us)
Async XLA Ops:
  7.2 345.0 %all-gather.3.cloned.1.call-start = ((), (), s32[]{:S(2)}) async-start(), calls=%async_computation.1 | async-start | bytes 16908288 | tf_op jit(solution)/shard_map/all_gather | solution.py:50
  10.6 13.9 %copy-start.5 = (s32[1,56,1]{1,2,0:T(1,128)S(1)}, s32[1,56,1]{1,2,0:T(1,128)}, u32[]{:S(2)}) copy-start(s32[1,56,1]{1,2,0:T(1,128)} %param.9) | copy-start | bytes 676
  10.6 14.0 %copy-start.6 = (s32[128]{0:T(128)S(1)}, s32[128]{0:T(128)}, u32[]{:S(2)}) copy-start(s32[128]{0:T(128)} %param.7) | copy-start | bytes 1540
  13.0 42.7 %all-to-all-start = ((bf16[56,128,128]{2,0,1:T(8,128)(2,1)}), bf16[56,128,128]{2,0,1:T(8,128)(2,1)S(1)}, u32[]{:S(2)}, u32[]{:S(2)}) async-start(bf16[56,128,128]{2,0,1:T(8,128)(2,1)} %copy.14), calls=%async_computation | async-start | bytes 3670016 | tf_op jit(solution)/shard_map/all_to_all | solution.py:41
  55.8 1.2 copy-start.3
  72.3 3.0 copy-start
  77.8 2.1 copy-start.1
  380.2 2.5 copy-start.2
  381.5 4.3 %copy-start.4 = (f32[4,16]{1,0:T(4,128)}, f32[4,16]{1,0:T(4,128)S(1)}, u32[]{:S(2)}) copy-start(f32[4,16]{1,0:T(4,128)S(1)} %bitcast_reduce_fusion) | copy-start | bytes 772
Sparse Core Ops, SparseCore 0:
  9.7 342.3 all-gather.2
where the time goes:
time: 395 us; the launch traced here: 393 us
  waiting for transfers between devices  302 us (76%)
  local copies, waits for them, and re-layouts  46.2 us (12%)
  other arithmetic  18.3 us (5%)
  between operations  14.2 us (4%)
  starting transfers between devices  11.5 us (3%)
    all_gather x1, waiting for transfers between devices, on_device(): lax.all_gather(attn_delta, ('expert', 'tensor'), axis=0, tiled=True)  271 us
    all_to_all x1, waiting for transfers between devices, on_device(): lax.all_to_all(outgoing, ('expert', 'tensor'), split_axis=1, concat_axis=...  31.2 us
    unnamed x16, local copies, waits for them, and re-layouts  27.5 us
    scatter x1, local copies, waits for them, and re-layouts, on_device(): placed = jnp.zeros_like(received).at[owner_block].set(received)  11.9 us
    all_to_all x1, starting transfers between devices, on_device(): lax.all_to_all(outgoing, ('expert', 'tensor'), split_axis=1, concat_axis=...  11.5 us
  transfers between devices with their start and end apart: 2, of which 2 were waited for; matrix products, arithmetic and copies ran while one was open for 7% of the time, Pallas kernels for 0%

commit v1 on v0

v1 whole, which is shorter than its diff:
```python
import functools

import jax
import jax.numpy as jnp
from jax import lax
from jax.experimental import pallas as pl
from jax.experimental.pallas import tpu as pltpu
from jax.sharding import PartitionSpec as P

MESH = pl.DeviceIdType.MESH
BLK = 128
F32 = jnp.float32
BF16 = jnp.bfloat16

OWNERS = 128
RB = 56
EXPERTS = 16
SHARES = 8
ROWS = OWNERS * RB
ATT_ROWS = 4
ATT_COLS = 2048
ATT_TILES = ATT_COLS // BLK
SUPER = 8
BLOCKS = 16
TILES = 7


def peer_at(e, t, k):
    s = lax.rem(k * 37, 128)
    x = lax.rem(e // 4 + s // 32, 4)
    y = lax.rem(lax.rem(t, 4) + lax.rem(s // 8, 4), 4)
    z = lax.rem((t // 4) * 2 + lax.rem(e // 2, 2) + lax.rem(s // 2, 4), 4)
    c = lax.rem(lax.rem(e, 2) + lax.rem(s, 2), 2)
    return x * 4 + lax.rem(z, 2) * 2 + c, (z // 2) * 4 + y


def exchange(
    delta, attn_delta, attn_shadow, expert_shadow,
    recv, shadow, attn_new, attn_codes, attn_amax,
    held, wide, send, gath, att_old, att_wide,
    load_sem, send_sem, recv_sem, a_send, a_recv, b_send, b_recv, c_send, c_recv,
):
    e = lax.axis_index("expert")
    t = lax.axis_index("tensor")
    me = e * SHARES + t

    barrier = pltpu.get_barrier_semaphore()

    def greet(k, _):
        p = lax.rem(me + k, OWNERS)
        pl.semaphore_signal(barrier, inc=1, device_id=(p // SHARES, lax.rem(p, SHARES)), device_id_type=MESH)
        return 0

    load_delta = pltpu.make_async_copy(delta.at[0], held, load_sem.at[0])
    load_delta.start()
    lax.fori_loop(1, OWNERS, greet, 0)
    own_rows = pltpu.make_async_copy(
        attn_delta.at[:, pl.ds(pl.multiple_of(t * ATT_COLS, ATT_COLS), ATT_COLS)], gath.at[me], load_sem.at[1]
    )
    own_rows.start()
    load_att = pltpu.make_async_copy(attn_shadow, att_old, load_sem.at[2])
    load_att.start()
    load_exp = pltpu.make_async_copy(expert_shadow.at[0], shadow, load_sem.at[3])
    load_exp.start()

    load_delta.wait()

    def widen(r, _):
        rows = held[r].astype(F32)
        for j in range(SHARES):
            wide[j, pl.ds(pl.multiple_of(r * EXPERTS, EXPERTS), EXPERTS), :] = rows[:, j * BLK:(j + 1) * BLK]
        return 0

    lax.fori_loop(0, RB, widen, 0, unroll=2)

    def block_of(pe, pt):
        return wide[pt, pl.ds(pe, RB, stride=EXPERTS), :].astype(BF16)

    recv[me] = block_of(e, t)

    pl.semaphore_wait(barrier, OWNERS - 1)

    for k in range(1, SHARES):
        q = lax.rem(t + k, SHARES)
        pltpu.make_async_remote_copy(
            src_ref=attn_delta.at[:, pl.ds(pl.multiple_of(q * ATT_COLS, ATT_COLS), ATT_COLS)],
            dst_ref=gath.at[me],
            send_sem=a_send,
            recv_sem=a_recv,
            device_id=(e, q),
            device_id_type=MESH,
        ).start()

    def send_block(k, _):
        pe, pt = peer_at(e, t, k)
        p = pe * SHARES + pt
        send[p] = block_of(pe, pt)
        pltpu.make_async_remote_copy(
            src_ref=send.at[p],
            dst_ref=recv.at[me],
            send_sem=send_sem,
            recv_sem=recv_sem,
            device_id=(pe, pt),
            device_id_type=MESH,
        ).start()
        return 0

    lax.fori_loop(1, 33, send_block, 0)

    own_rows.wait()
    pltpu.make_async_copy(gath.at[pl.ds(0, 7)], gath.at[pl.ds(0, 7)], a_recv).wait()

    core = lax.rem(e, 2)

    def chunk(i):
        return gath.at[pl.ds(pl.multiple_of(i * SHARES, SHARES), SHARES)]

    def to_chip(h):
        return pltpu.make_async_remote_copy(
            src_ref=chunk(e), dst_ref=chunk(e), send_sem=b_send.at[h], recv_sem=b_recv.at[h],
            device_id=(lax.rem(e + 2 * h, EXPERTS), t), device_id_type=MESH,
        )

    def to_core(h):
        src = lax.rem(e + EXPERTS - 2 * h, EXPERTS)
        return pltpu.make_async_remote_copy(
            src_ref=chunk(src), dst_ref=chunk(src), send_sem=c_send.at[h], recv_sem=c_recv.at[h],
            device_id=(e + 1 - 2 * core, t), device_id_type=MESH,
        )

    to_core(0).start()
    for h in range(1, 8):
        to_chip(h).start()

    lax.fori_loop(33, OWNERS, send_block, 0)

    for h in range(1, 8):
        to_chip(h).wait_recv()
        to_core(h).start()
    for h in range(8):
        to_core(h).wait_recv()

    load_att.wait()
    for i in range(OWNERS):
        att_wide[i // 2, (i % 2) * 4:(i % 2) * 4 + 4, :] = gath[i].astype(F32)

    def att_tile_row(i, _):
        tops = []
        for j in range(ATT_TILES):
            cols = slice(j * BLK, (j + 1) * BLK)
            groups = pl.ds(i * 16, 16)
            new = att_old[groups, :, cols] + att_wide[groups, :, cols]
            attn_new[groups, :, cols] = new
            top = jnp.max(jnp.max(jnp.max(jnp.abs(new), axis=0), axis=0, keepdims=True), axis=1, keepdims=True)
            codes = new * (1.0 / (top + 1e-6))[None]
            attn_codes[pl.ds(pl.multiple_of(i * BLK, BLK), BLK), cols] = codes.reshape(BLK, BLK).astype(BF16)
            tops.append(jnp.broadcast_to(top, (1, BLK)))
        lane = lax.broadcasted_iota(jnp.int32, (1, BLK), 1)
        row = jnp.zeros((1, BLK), F32)
        for j in range(ATT_TILES):
            row = jnp.where(lane == j, tops[j], row)
        attn_amax[pl.ds(i, 1), :] = row
        return 0

    lax.fori_loop(0, 4, att_tile_row, 0)

    load_exp.wait()
    pltpu.make_async_copy(gath.at[pl.ds(0, 7)], gath.at[pl.ds(0, 7)], a_send).wait()
    for h in range(1, 8):
        to_chip(h).wait_send()
    for h in range(8):
        to_core(h).wait_send()
    whole = pl.ds(0, OWNERS - 1)
    pltpu.make_async_copy(send.at[whole], send.at[whole], send_sem).wait()
    pltpu.make_async_copy(recv.at[whole], recv.at[whole], recv_sem).wait()


def finish(
    owner, mode, recv, shadow, att_new_v, att_codes_v, att_amax_v,
    expert_new, expert_codes, expert_amax, attn_new, attn_codes, attn_amax,
    place, new_v, codes_v, amax_v, att_small, out_sem, new_sem, codes_sem,
):
    copy_an = pltpu.make_async_copy(att_new_v, attn_new, out_sem.at[0])
    copy_ac = pltpu.make_async_copy(att_codes_v, attn_codes, out_sem.at[1])

    def invert(l, _):
        place[owner[l]] = l
        return 0

    lax.fori_loop(0, OWNERS, invert, 0, unroll=8)

    def group_rows(s):
        return pl.ds(pl.multiple_of(s * (BLOCKS * RB), BLOCKS * RB), BLOCKS * RB)

    def copy_new(s):
        return pltpu.make_async_copy(new_v.at[group_rows(s)], expert_new.at[0, group_rows(s)], new_sem)

    def copy_codes(s):
        return pltpu.make_async_copy(codes_v.at[group_rows(s)], expert_codes.at[0, group_rows(s)], codes_sem)

    def group(s, _):
        for j in range(BLOCKS):
            rows = pl.ds(pl.multiple_of((s * BLOCKS + j) * RB, 8), RB)
            new_v[rows, :] = shadow[rows, :] + recv[place[s * BLOCKS + j]].astype(F32)
        copy_new(s).start()
        for j in range(TILES):
            i = s * TILES + j
            rows = pl.ds(pl.multiple_of(i * BLK, BLK), BLK)
            tile = new_v[rows, :]
            column = jnp.max(jnp.abs(tile), axis=0, keepdims=True)
            top = jnp.max(column, axis=1, keepdims=True)
            chosen = jnp.where(mode[i] == 0, jnp.broadcast_to(top, column.shape), column)
            amax_v[pl.ds(i, 1), :] = chosen
            codes_v[rows, :] = (tile * (1.0 / (chosen + 1e-6))).astype(BF16)
        copy_codes(s).start()
        return 0

    copy_an.start()
    copy_ac.start()
    lax.fori_loop(0, SUPER, group, 0)
    att_small[...] = att_amax_v[:, :ATT_TILES]
    copy_am = pltpu.make_async_copy(amax_v, expert_amax.at[0], out_sem.at[2])
    copy_am.start()
    copy_aa = pltpu.make_async_copy(att_small, attn_amax, out_sem.at[3])
    copy_aa.start()
    copy_an.wait()
    copy_ac.wait()
    copy_am.wait()
    copy_aa.wait()
    pltpu.make_async_copy(new_v, expert_new.at[0], new_sem).wait()
    pltpu.make_async_copy(codes_v, expert_codes.at[0], codes_sem).wait()


def on_device(learner_delta, owner_block, expert_shadow, tile_mode, attn_delta, attn_shadow):
    vmem = pl.BlockSpec(memory_space=pltpu.VMEM)
    hbm = pl.BlockSpec(memory_space=pltpu.HBM)
    smem = pl.BlockSpec(memory_space=pltpu.SMEM)
    dma = pltpu.SemaphoreType.DMA
    shape = jax.ShapeDtypeStruct
    recv, shadow, att_new_v, att_codes_v, att_amax_v = pl.pallas_call(
        exchange,
        name="exchange",
        out_shape=(
            shape((OWNERS, RB, BLK), BF16),
            shape((ROWS, BLK), F32),
            shape((64, 8, ATT_COLS), F32),
            shape((512, ATT_COLS), BF16),
            shape((4, BLK), F32),
        ),
        in_specs=[hbm] * 4,
        out_specs=(vmem,) * 5,
        scratch_shapes=[
            pltpu.VMEM((RB, EXPERTS, 1024), BF16),
            pltpu.VMEM((SHARES, RB * EXPERTS, BLK), F32),
            pltpu.VMEM((OWNERS, RB, BLK), BF16),
            pltpu.VMEM((OWNERS, ATT_ROWS, ATT_COLS), BF16),
            pltpu.VMEM((64, 8, ATT_COLS), F32),
            pltpu.VMEM((64, 8, ATT_COLS), F32),
            dma((4,)), dma(()), dma(()), dma(()), dma(()),
            dma((8,)), dma((8,)), dma((8,)), dma((8,)),
        ],
        compiler_params=pltpu.CompilerParams(
            collective_id=0, has_side_effects=True, vmem_limit_bytes=40 << 20
        ),
    )(learner_delta, attn_delta, attn_shadow.reshape(64, 8, ATT_COLS), expert_shadow)

    return pl.pallas_call(
        finish,
        name="finish",
        out_shape=(
            shape((1, ROWS, BLK), F32),
            shape((1, ROWS, BLK), BF16),
            shape((1, ROWS // BLK, BLK), F32),
            shape((512, ATT_COLS), F32),
            shape((512, ATT_COLS), BF16),
            shape((4, ATT_TILES), F32),
        ),
        in_specs=[smem, smem] + [vmem] * 5,
        out_specs=(hbm,) * 6,
        scratch_shapes=[
            pltpu.SMEM((OWNERS,), jnp.int32),
            pltpu.VMEM((ROWS, BLK), F32),
            pltpu.VMEM((ROWS, BLK), BF16),
            pltpu.VMEM((ROWS // BLK, BLK), F32),
            pltpu.VMEM((4, ATT_TILES), F32),
            dma((4,)), dma(()), dma(()),
        ],
        compiler_params=pltpu.CompilerParams(vmem_limit_bytes=40 << 20),
    )(owner_block, tile_mode.reshape(ROWS // BLK), recv, shadow, att_new_v.reshape(512, ATT_COLS), att_codes_v, att_amax_v)


def solution(mesh):
    return jax.shard_map(
        on_device,
        mesh=mesh,
        in_specs=(
            P(("expert", "tensor"), None, None, None),
            P(),
            P("expert", None, "tensor"),
            P("expert", None, "tensor"),
            P(("expert", "tensor"), None),
            P(None, "tensor"),
        ),
        out_specs=(
            P("expert", None, "tensor"),
            P("expert", None, "tensor"),
            P("expert", None, "tensor"),
            P(None, "tensor"),
            P(None, "tensor"),
            P(None, "tensor"),
        ),
        check_vma=False,
    )
```

time: 395 us -> 64.1 us (0.16)
  waiting for transfers between devices: 302 us -> 0 us
  Pallas kernels: 0 us -> 56.2 us
  local copies, waits for them, and re-layouts: 46.2 us -> 6.62 us
  other arithmetic: 18.3 us -> 0 us
  between operations: 14.2 us -> 0.68 us
  starting transfers between devices: 11.5 us -> 0 us
    all_gather x1 -> x0, waiting for transfers between devices: 271 us -> none  [on_device(): lax.all_gather(attn_delta, ('expert', 'tensor'), axis=0, tiled=True)]
    pallas_call x0 -> x2, Pallas kernels: none -> 56.2 us  [the longest x1 51.1 us: on_device(): pl.pallas_call(exchange, name='exchange', out_shape=(shape((OWNERS, RB, B...]
    all_to_all x1 -> x0, waiting for transfers between devices: 31.2 us -> none  [on_device(): lax.all_to_all(outgoing, ('expert', 'tensor'), split_axis=1, concat_axis=...]
    unnamed x16 -> x12, local copies, waits for them, and re-layouts: 27.5 us -> 6.62 us
    scatter x1 -> x0, local copies, waits for them, and re-layouts: 11.9 us -> none  [on_device(): placed = jnp.zeros_like(received).at[owner_block].set(received)]
    all_to_all x1 -> x0, starting transfers between devices: 11.5 us -> none  [on_device(): lax.all_to_all(outgoing, ('expert', 'tensor'), split_axis=1, concat_axis=...]
    reduce_max x4 -> x0, other arithmetic: 6 us -> none  [the longest x2 3.21 us: expert_quantize(): column_max.reshape(count_lead, count_rows // BLK, count_cols // BLK, BLK)]
    another operation x2 -> x0, local copies, waits for them, and re-layouts: 5.12 us -> none  [on_device(): learner_piece.reshape(block_rows, expert_count * tensor_count, column_share)]
  transfers between devices with their start and end apart: 2 -> 0, of which waited for: 2 -> 0; matrix products, arithmetic and copies ran while one was open for 7% -> 0% of each run, Pallas kernels for 0% -> 0%
where the time goes in v1:
time: 64.1 us; the launch traced here: 63.5 us
  Pallas kernels  56.2 us (88%)
  local copies, waits for them, and re-layouts  6.62 us (10%)
  between operations  0.68 us (1%)
    pallas_call x1, Pallas kernels, on_device(): pl.pallas_call(exchange, name='exchange', out_shape=(shape((OWNERS, RB, B...  51.1 us
    unnamed x12, local copies, waits for them, and re-layouts  6.62 us
    pallas_call x1, Pallas kernels, on_device(): pl.pallas_call(finish, name='finish', out_shape=(shape((1, ROWS, BLK), F3...  5.1 us

profile of v1, /device:TPU:1, one launch (start us, length us, event | category | flops | bytes accessed | tf_op | source)
XLA Modules:
  0.0 63.5 jit_solution(17850256952413350559)
XLA Ops:
  0.6 0.0 copy-start.1
  0.6 2.0 %copy-done.1 = f32[1,7168,128]{2,1,0:T(8,128)S(1)} copy-done((f32[1,7168,128]{2,1,0:T(8,128)S(1)}, f32[1,7168,128]{2,1,0:T(8,128)}, u32[]{:S(2)}) %copy-start.1) | copy-done | bytes 3670040
  2.7 0.0 copy-start.2
  2.7 1.5 %copy-done.2 = bf16[1,56,16,1024]{3,2,1,0:T(8,128)(2,1)S(1)} copy-done((bf16[1,56,16,1024]{3,2,1,0:T(8,128)(2,1)S(1)}, bf16[1,56,16,1024]{3,2,1,0:T(8,128)(2,1)}, u32[]{:S(2)}) %copy-start.2) | copy-done | bytes 1835032
  4.2 0.0 copy-start.3
  4.2 0.9 %copy-done.3 = bf16[4,16384]{1,0:T(4,128)(2,1)S(1)} copy-done((bf16[4,16384]{1,0:T(4,128)(2,1)S(1)}, bf16[4,16384]{1,0:T(4,128)(2,1)}, u32[]{:S(2)}) %copy-start.3) | copy-done | bytes 131096
  5.1 0.0 copy-start.4
  5.1 0.0 copy-start.5
  5.1 51.1 %exchange.1 = (bf16[128,56,128]{2,1,0:T(8,128)(2,1)S(1)}, f32[7168,128]{1,0:T(8,128)S(1)}, f32[64,8,2048]{2,1,0:T(8,128)}, bf16[512,2048]{1,0:T(8,128)(2,1)S(1)}, f32[4,128]{1,0:T(4,128)S(1)}) custom-call(bf16[1,56,16,1024]{3,2,1,0:T(8,128)(2,1)S(1)} %copy-done.2, bf16[4,16384]{1,0:T(4,128)(2,1)S(1)} %copy-done.3, f32[64,8,2048]{2,1,0:T(8,128)} %bitcast.5, ...), custom_call_target="tpu_custom_call" | custom-call | tf_op jit(solution)/shard_map/exchange/pallas_call | solution.py:240
  56.2 0.0 copy-done.4
  56.2 0.0 copy-done.5
  56.2 0.0 copy-start
  56.2 2.2 %copy-done = f32[64,8,2048]{2,1,0:T(8,128)S(1)} copy-done((f32[64,8,2048]{2,1,0:T(8,128)S(1)}, f32[64,8,2048]{2,1,0:T(8,128)}, u32[]{:S(2)}) %copy-start) | copy-done | bytes 4194328
  58.4 5.1 %finish.1 = (f32[1,7168,128]{2,1,0:T(8,128)}, bf16[1,7168,128]{2,1,0:T(8,128)(2,1)}, f32[1,56,128]{2,1,0:T(8,128)}, f32[512,2048]{1,0:T(8,128)}, bf16[512,2048]{1,0:T(8,128)(2,1)}, /*index=5*/f32[4,16]{1,0:T(4,128)}) custom-call(s32[128]{0:T(128)S(1)} %copy-done.4, s32[56]{0:T(128)S(1)} %bitcast.4, bf16[128,56,128]{2,1,0:T(8,128)(2,1)S(1)} %get-tuple-element.11.recv, ...), custom_call_target="tpu_custom_call" | custom-call | tf_op jit(solution)/shard_map/finish/pallas_call | solution.py:267
Async XLA Ops:
  0.6 2.0 %copy-start.1 = (f32[1,7168,128]{2,1,0:T(8,128)S(1)}, f32[1,7168,128]{2,1,0:T(8,128)}, u32[]{:S(2)}) copy-start(f32[1,7168,128]{2,1,0:T(8,128)} %expert_shadow.1) | copy-start | bytes 11010052
  2.7 1.5 %copy-start.2 = (bf16[1,56,16,1024]{3,2,1,0:T(8,128)(2,1)S(1)}, bf16[1,56,16,1024]{3,2,1,0:T(8,128)(2,1)}, u32[]{:S(2)}) copy-start(bf16[1,56,16,1024]{3,2,1,0:T(8,128)(2,1)} %delta.1) | copy-start | bytes 5505028
  4.2 0.9 %copy-start.3 = (bf16[4,16384]{1,0:T(4,128)(2,1)S(1)}, bf16[4,16384]{1,0:T(4,128)(2,1)}, u32[]{:S(2)}) copy-start(bf16[4,16384]{1,0:T(4,128)(2,1)} %attn_delta.1) | copy-start | bytes 393220
  5.1 51.1 %copy-start.4 = (s32[128]{0:T(128)S(1)}, s32[128]{0:T(128)}, u32[]{:S(2)}) copy-start(s32[128]{0:T(128)} %owner.1) | copy-start | bytes 1540
  5.1 51.1 %copy-start.5 = (s32[1,56,1]{1,2,0:T(1,128)S(1)}, s32[1,56,1]{1,2,0:T(1,128)}, u32[]{:S(2)}) copy-start(s32[1,56,1]{1,2,0:T(1,128)} %param.9) | copy-start | bytes 676
  56.2 2.2 %copy-start = (f32[64,8,2048]{2,1,0:T(8,128)S(1)}, f32[64,8,2048]{2,1,0:T(8,128)}, u32[]{:S(2)}) copy-start(f32[64,8,2048]{2,1,0:T(8,128)} %get-tuple-element.13) | copy-start | bytes 12582916

commit v2 on v1

--- a/solution.py
+++ b/solution.py
@@ -25,42 +25,72 @@
 TILES = 7
 
 
-def peer_at(e, t, k):
-    s = lax.rem(k * 37, 128)
-    x = lax.rem(e // 4 + s // 32, 4)
-    y = lax.rem(lax.rem(t, 4) + lax.rem(s // 8, 4), 4)
-    z = lax.rem((t // 4) * 2 + lax.rem(e // 2, 2) + lax.rem(s // 2, 4), 4)
-    c = lax.rem(lax.rem(e, 2) + lax.rem(s, 2), 2)
-    return x * 4 + lax.rem(z, 2) * 2 + c, (z // 2) * 4 + y
+WIDE_Z = 1024
+WIDE_X = ATT_COLS - WIDE_Z
+AHEAD, BETWEEN = 40, 3
+
+
+def hops(s):
+    return sum(min(d, 4 - d) for d in (s // 16, s // 4 % 4, s % 4))
+
+
+TABLE = sorted(((37 * k) % 64 for k in range(64)), key=lambda s: -hops(s))
+WORDS = [sum(s << (6 * n) for n, s in enumerate(TABLE[4 * w:4 * w + 4])) for w in range(16)]
+
+
+def chip_offset(i):
+    word = jnp.int32(WORDS[0])
+    for w in range(1, 16):
+        word = jnp.where(lax.div(i, 4) == w, WORDS[w], word)
+    s = lax.rem(word, 64)
+    for n in range(1, 4):
+        s = jnp.where(lax.rem(i, 4) == n, lax.rem(lax.div(word, 64 ** n), 64), s)
+    return lax.div(s, 16), lax.rem(lax.div(s, 4), 4), lax.rem(s, 4)
 
 
 def exchange(
     delta, attn_delta, attn_shadow, expert_shadow,
     recv, shadow, attn_new, attn_codes, attn_amax,
-    held, wide, send, gath, att_old, att_wide,
-    load_sem, send_sem, recv_sem, a_send, a_recv, b_send, b_recv, c_send, c_recv,
+    held, wide, send, by_z, by_x, other, att_old, att_wide,
+    load_sem, send_sem, recv_sem, first_send, first_recv, second_send, second_recv, last_send, last_recv,
 ):
     e = lax.axis_index("expert")
     t = lax.axis_index("tensor")
     me = e * SHARES + t
-
-    barrier = pltpu.get_barrier_semaphore()
-
-    def greet(k, _):
-        p = lax.rem(me + k, OWNERS)
-        pl.semaphore_signal(barrier, inc=1, device_id=(p // SHARES, lax.rem(p, SHARES)), device_id_type=MESH)
-        return 0
+    x, y, core = lax.div(e, 4), lax.rem(t, 4), lax.rem(e, 2)
+    high, low = lax.div(t, 4), lax.rem(lax.div(e, 2), 2)
+    z = high * 2 + low
+
+    def step(v, d):
+        return lax.rem(v + d, 4)
+
+    def at(x, y, z, core):
+        return x * 4 + lax.rem(z, 2) * 2 + core, lax.div(z, 2) * 4 + y
 
     load_delta = pltpu.make_async_copy(delta.at[0], held, load_sem.at[0])
     load_delta.start()
-    lax.fori_loop(1, OWNERS, greet, 0)
-    own_rows = pltpu.make_async_copy(
-        attn_delta.at[:, pl.ds(pl.multiple_of(t * ATT_COLS, ATT_COLS), ATT_COLS)], gath.at[me], load_sem.at[1]
+
+    barrier = pltpu.get_barrier_semaphore()
+    for de in range(EXPERTS):
+        for dt in range(SHARES):
+            if de or dt:
+                pl.semaphore_signal(
+                    barrier, inc=1, device_id=(lax.rem(e + de, EXPERTS), lax.rem(t + dt, SHARES)), device_id_type=MESH
+                )
+
+    def columns(high, y, first, count):
+        return attn_delta.at[:, pl.ds(pl.multiple_of((high * 4 + y) * ATT_COLS + first, BLK), count)]
+
+    own = (
+        pltpu.make_async_copy(columns(high, y, 0, WIDE_Z), by_z.at[core, x, z * 4 + y], load_sem.at[1]),
+        pltpu.make_async_copy(columns(1 - high, y, 0, WIDE_Z), other.at[x * 4 + y], load_sem.at[2]),
+        pltpu.make_async_copy(columns(high, y, WIDE_Z, WIDE_X), by_x.at[core, x, z * 4 + y], load_sem.at[3]),
     )
-    own_rows.start()
-    load_att = pltpu.make_async_copy(attn_shadow, att_old, load_sem.at[2])
+    for copy in own:
+        copy.start()
+    load_att = pltpu.make_async_copy(attn_shadow, att_old, load_sem.at[4])
     load_att.start()
-    load_exp = pltpu.make_async_copy(expert_shadow.at[0], shadow, load_sem.at[3])
+    load_exp = pltpu.make_async_copy(expert_shadow.at[0], shadow, load_sem.at[5])
     load_exp.start()
 
     load_delta.wait()
@@ -80,19 +110,25 @@
 
     pl.semaphore_wait(barrier, OWNERS - 1)
 
-    for k in range(1, SHARES):
-        q = lax.rem(t + k, SHARES)
+    plane = sorted((k for k in range(1, 16)), key=lambda k: -hops(k))
+    for k in plane:
+        a, b = k // 4, k % 4
+        to = at(step(x, a), step(y, b), z, core)
+        for n, (share, dst) in enumerate(((high, by_z.at[core, x, z * 4 + y]), (1 - high, other.at[x * 4 + y]))):
+            pltpu.make_async_remote_copy(
+                src_ref=columns(share, step(y, b), 0, WIDE_Z), dst_ref=dst,
+                send_sem=first_send.at[n], recv_sem=first_recv.at[n], device_id=to, device_id_type=MESH,
+            ).start()
+        there = step(z, a)
         pltpu.make_async_remote_copy(
-            src_ref=attn_delta.at[:, pl.ds(pl.multiple_of(q * ATT_COLS, ATT_COLS), ATT_COLS)],
-            dst_ref=gath.at[me],
-            send_sem=a_send,
-            recv_sem=a_recv,
-            device_id=(e, q),
-            device_id_type=MESH,
+            src_ref=columns(lax.div(there, 2), step(y, b), WIDE_Z, WIDE_X), dst_ref=by_x.at[core, x, z * 4 + y],
+            send_sem=first_send.at[2], recv_sem=first_recv.at[2],
+            device_id=at(x, step(y, b), there, core), device_id_type=MESH,
         ).start()
 
     def send_block(k, _):
-        pe, pt = peer_at(e, t, k)
+        dx, dy, dz = chip_offset(lax.div(k, 2))
+        pe, pt = at(step(x, dx), step(y, dy), step(z, dz), lax.rem(core + 1 - lax.rem(k, 2), 2))
         p = pe * SHARES + pt
         send[p] = block_of(pe, pt)
         pltpu.make_async_remote_copy(
@@ -105,44 +141,72 @@
         ).start()
         return 0
 
-    lax.fori_loop(1, 33, send_block, 0)
-
-    own_rows.wait()
-    pltpu.make_async_copy(gath.at[pl.ds(0, 7)], gath.at[pl.ds(0, 7)], a_recv).wait()
-
-    core = lax.rem(e, 2)
-
-    def chunk(i):
-        return gath.at[pl.ds(pl.multiple_of(i * SHARES, SHARES), SHARES)]
-
-    def to_chip(h):
+    lax.fori_loop(0, AHEAD, send_block, 0)
+
+    for copy in own:
+        copy.wait()
+    landed = (by_z.at[0, 0, pl.ds(0, 15)], other.at[pl.ds(0, 15)], by_x.at[0, 0, pl.ds(0, 15)])
+    for n, ref in enumerate(landed):
+        pltpu.make_async_copy(ref, ref, first_recv.at[n]).wait()
+
+    def along_z(r, d, src=None):
+        i, there = step(x, r), step(z, d)
+        dst = by_z.at[core, i, pl.ds(z * 4, 4)]
         return pltpu.make_async_remote_copy(
-            src_ref=chunk(e), dst_ref=chunk(e), send_sem=b_send.at[h], recv_sem=b_recv.at[h],
-            device_id=(lax.rem(e + 2 * h, EXPERTS), t), device_id_type=MESH,
+            src_ref=dst if src is None else src, dst_ref=dst,
+            send_sem=second_send.at[r, d], recv_sem=second_recv.at[r, d],
+            device_id=at(x, y, there, core), device_id_type=MESH,
         )
 
-    def to_core(h):
-        src = lax.rem(e + EXPERTS - 2 * h, EXPERTS)
+    def start_z(r, d):
+        same = lax.div(step(z, d), 2) == high
+
+        @pl.when(same)
+        def _():
+            along_z(r, d).start()
+
+        @pl.when(jnp.logical_not(same))
+        def _():
+            along_z(r, d, other.at[pl.ds(step(x, r) * 4, 4)]).start()
+
+    def along_x(r):
+        ref = by_x.at[core, x]
         return pltpu.make_async_remote_copy(
-            src_ref=chunk(src), dst_ref=chunk(src), send_sem=c_send.at[h], recv_sem=c_recv.at[h],
-            device_id=(e + 1 - 2 * core, t), device_id_type=MESH,
+            src_ref=ref, dst_ref=ref, send_sem=second_send.at[r, 0], recv_sem=second_recv.at[r, 0],
+            device_id=at(step(x, 4 - r), y, z, core), device_id_type=MESH,
         )
 
-    to_core(0).start()
-    for h in range(1, 8):
-        to_chip(h).start()
-
-    lax.fori_loop(33, OWNERS, send_block, 0)
-
-    for h in range(1, 8):
-        to_chip(h).wait_recv()
-        to_core(h).start()
-    for h in range(8):
-        to_core(h).wait_recv()
-
-    load_att.wait()
-    for i in range(OWNERS):
-        att_wide[i // 2, (i % 2) * 4:(i % 2) * 4 + 4, :] = gath[i].astype(F32)
+    def across(n, r):
+        ref = (by_z, by_x)[n].at[core, step(x, r)]
+        return pltpu.make_async_remote_copy(
+            src_ref=ref, dst_ref=ref, send_sem=last_send.at[n, r], recv_sem=last_recv.at[n, r],
+            device_id=at(x, y, z, 1 - core), device_id_type=MESH,
+        )
+
+    starts = []
+    for r in range(4):
+        starts += [functools.partial(start_z, r, d) for d in (2, 1, 3)]
+        if r:
+            starts.append(along_x(r).start)
+    k = AHEAD
+    for start in starts:
+        start()
+        upto = min(k + BETWEEN, OWNERS - 1)
+        if upto > k:
+            lax.fori_loop(k, upto, send_block, 0)
+            k = upto
+    lax.fori_loop(k, OWNERS - 1, send_block, 0)
+
+    def att_widen(m, _):
+        i, j = lax.div(m, 4), lax.rem(m, 4)
+        gx, gc = lax.div(i, 4), lax.rem(i, 2)
+        gz = lax.div(j, 2) * 2 + lax.rem(lax.div(i, 2), 2)
+        for n in range(2):
+            owner = gz * 4 + lax.rem(j, 2) * 2 + n
+            rows = slice(4 * n, 4 * n + 4)
+            att_wide[m, rows, :WIDE_Z] = by_z[gc, gx, owner].astype(F32)
+            att_wide[m, rows, WIDE_Z:] = by_x[gc, gx, owner].astype(F32)
+        return 0
 
     def att_tile_row(i, _):
         tops = []
@@ -162,14 +226,39 @@
         attn_amax[pl.ds(i, 1), :] = row
         return 0
 
-    lax.fori_loop(0, 4, att_tile_row, 0)
+    load_att.wait()
+
+    def arrive(r):
+        for d in (1, 3, 2):
+            along_z(r, d).wait_recv()
+        across(0, r).start()
+        if r:
+            along_x(r).wait_recv()
+        across(1, r).start()
+
+    def work(r):
+        across(0, r).wait_recv()
+        across(1, r).wait_recv()
+        i = step(x, r)
+        lax.fori_loop(i * 16, i * 16 + 16, att_widen, 0)
+        att_tile_row(i, 0)
+
+    for r in range(5):
+        if r < 4:
+            arrive(r)
+        if r:
+            work(r - 1)
 
     load_exp.wait()
-    pltpu.make_async_copy(gath.at[pl.ds(0, 7)], gath.at[pl.ds(0, 7)], a_send).wait()
-    for h in range(1, 8):
-        to_chip(h).wait_send()
-    for h in range(8):
-        to_core(h).wait_send()
+    for n, ref in enumerate(landed):
+        pltpu.make_async_copy(ref, ref, first_send.at[n]).wait()
+    for r in range(4):
+        for d in (1, 2, 3):
+            along_z(r, d).wait_send()
+        if r:
+            along_x(r).wait_send()
+        for n in range(2):
+            across(n, r).wait_send()
     whole = pl.ds(0, OWNERS - 1)
     pltpu.make_async_copy(send.at[whole], send.at[whole], send_sem).wait()
     pltpu.make_async_copy(recv.at[whole], recv.at[whole], recv_sem).wait()
@@ -237,15 +326,16 @@
     smem = pl.BlockSpec(memory_space=pltpu.SMEM)
     dma = pltpu.SemaphoreType.DMA
     shape = jax.ShapeDtypeStruct
+    in_hbm = functools.partial(pltpu.with_memory_space_constraint, memory_space=pltpu.HBM)
     recv, shadow, att_new_v, att_codes_v, att_amax_v = pl.pallas_call(
         exchange,
         name="exchange",
         out_shape=(
-            shape((OWNERS, RB, BLK), BF16),
-            shape((ROWS, BLK), F32),
-            shape((64, 8, ATT_COLS), F32),
-            shape((512, ATT_COLS), BF16),
-            shape((4, BLK), F32),
+            pltpu.VMEM((OWNERS, RB, BLK), BF16),
+            pltpu.VMEM((ROWS, BLK), F32),
+            pltpu.VMEM((64, 8, ATT_COLS), F32),
+            pltpu.VMEM((512, ATT_COLS), BF16),
+            pltpu.VMEM((4, BLK), F32),
         ),
         in_specs=[hbm] * 4,
         out_specs=(vmem,) * 5,
@@ -253,16 +343,20 @@
             pltpu.VMEM((RB, EXPERTS, 1024), BF16),
             pltpu.VMEM((SHARES, RB * EXPERTS, BLK), F32),
             pltpu.VMEM((OWNERS, RB, BLK), BF16),
-            pltpu.VMEM((OWNERS, ATT_ROWS, ATT_COLS), BF16),
+            pltpu.VMEM((2, 4, 16, ATT_ROWS, WIDE_Z), BF16),
+            pltpu.VMEM((2, 4, 16, ATT_ROWS, WIDE_X), BF16),
+            pltpu.VMEM((16, ATT_ROWS, WIDE_Z), BF16),
             pltpu.VMEM((64, 8, ATT_COLS), F32),
             pltpu.VMEM((64, 8, ATT_COLS), F32),
-            dma((4,)), dma(()), dma(()), dma(()), dma(()),
-            dma((8,)), dma((8,)), dma((8,)), dma((8,)),
+            dma((6,)), dma(()), dma(()),
+            dma((3,)), dma((3,)),
+            dma((4, 4)), dma((4, 4)),
+            dma((2, 4)), dma((2, 4)),
         ],
         compiler_params=pltpu.CompilerParams(
             collective_id=0, has_side_effects=True, vmem_limit_bytes=40 << 20
         ),
-    )(learner_delta, attn_delta, attn_shadow.reshape(64, 8, ATT_COLS), expert_shadow)
+    )(*(in_hbm(x) for x in (learner_delta, attn_delta, attn_shadow.reshape(64, 8, ATT_COLS), expert_shadow)))
 
     return pl.pallas_call(
         finish,

time: 64.1 us -> 50.9 us (0.79)
  local copies, waits for them, and re-layouts: 6.62 us -> 0.01 us
  Pallas kernels: 56.2 us -> 50.1 us
    unnamed x12 -> x4, local copies, waits for them, and re-layouts: 6.62 us -> 0.01 us
    pallas_call x1, Pallas kernels: 51.1 us -> 45 us  [on_device(): pl.pallas_call(exchange, name='exchange', out_shape=(pltpu.VMEM((OWNERS,...]
where the time goes in v2:
time: 50.9 us; the launch traced here: 50.8 us
  Pallas kernels  50.1 us (98%)
  between operations  0.67 us (1%)
    pallas_call x1, Pallas kernels, on_device(): pl.pallas_call(exchange, name='exchange', out_shape=(pltpu.VMEM((OWNERS,...  45 us
    pallas_call x1, Pallas kernels, on_device(): pl.pallas_call(finish, name='finish', out_shape=(shape((1, ROWS, BLK), F3...  5.11 us

profile of v2, /device:TPU:1, one launch (start us, length us, event | category | flops | bytes accessed | tf_op | source)
XLA Modules:
  0.0 50.8 jit_solution(11622382735224716013)
XLA Ops:
  0.6 0.0 copy-start
  0.6 0.0 copy-start.1
  0.7 45.0 %exchange.1 = (bf16[128,56,128]{2,1,0:T(8,128)(2,1)S(1)}, f32[7168,128]{1,0:T(8,128)S(1)}, f32[64,8,2048]{2,1,0:T(8,128)S(1)}, bf16[512,2048]{1,0:T(8,128)(2,1)S(1)}, f32[4,128]{1,0:T(4,128)S(1)}) custom-call(bf16[1,56,16,1024]{3,2,1,0:T(8,128)(2,1)} %delta.1, bf16[4,16384]{1,0:T(4,128)(2,1)} %attn_delta.1, f32[64,8,2048]{2,1,0:T(8,128)} %bitcast.5, ...), custom_call_target="tpu_custom_call" | custom-call | tf_op jit(solution)/shard_map/exchange/pallas_call | solution.py:330
  45.6 0.0 copy-done
  45.7 0.0 copy-done.1
  45.7 5.1 %finish.1 = (f32[1,7168,128]{2,1,0:T(8,128)}, bf16[1,7168,128]{2,1,0:T(8,128)(2,1)}, f32[1,56,128]{2,1,0:T(8,128)}, f32[512,2048]{1,0:T(8,128)}, bf16[512,2048]{1,0:T(8,128)(2,1)}, /*index=5*/f32[4,16]{1,0:T(4,128)}) custom-call(s32[128]{0:T(128)S(1)} %copy-done, s32[56]{0:T(128)S(1)} %bitcast.4, bf16[128,56,128]{2,1,0:T(8,128)(2,1)S(1)} %get-tuple-element.11.recv, ...), custom_call_target="tpu_custom_call" | custom-call | tf_op jit(solution)/shard_map/finish/pallas_call | solution.py:361
Async XLA Ops:
  0.6 45.0 %copy-start = (s32[128]{0:T(128)S(1)}, s32[128]{0:T(128)}, u32[]{:S(2)}) copy-start(s32[128]{0:T(128)} %owner.1) | copy-start | bytes 1540
  0.6 45.0 %copy-start.1 = (s32[1,56,1]{1,2,0:T(1,128)S(1)}, s32[1,56,1]{1,2,0:T(1,128)}, u32[]{:S(2)}) copy-start(s32[1,56,1]{1,2,0:T(1,128)} %param.9) | copy-start | bytes 676

commit v3 on v1

--- a/solution.py
+++ b/solution.py
@@ -25,39 +25,48 @@
 TILES = 7
 
 
-def peer_at(e, t, k):
-    s = lax.rem(k * 37, 128)
-    x = lax.rem(e // 4 + s // 32, 4)
-    y = lax.rem(lax.rem(t, 4) + lax.rem(s // 8, 4), 4)
-    z = lax.rem((t // 4) * 2 + lax.rem(e // 2, 2) + lax.rem(s // 2, 4), 4)
-    c = lax.rem(lax.rem(e, 2) + lax.rem(s, 2), 2)
-    return x * 4 + lax.rem(z, 2) * 2 + c, (z // 2) * 4 + y
+AHEAD, BETWEEN, UPTO = 50, 4, 90
+STRIDE = 21
 
 
 def exchange(
     delta, attn_delta, attn_shadow, expert_shadow,
     recv, shadow, attn_new, attn_codes, attn_amax,
     held, wide, send, gath, att_old, att_wide,
-    load_sem, send_sem, recv_sem, a_send, a_recv, b_send, b_recv, c_send, c_recv,
+    load_sem, send_sem, recv_sem, first_send, first_recv, second_send, second_recv, third_send, third_recv,
+    last_send, last_recv,
 ):
     e = lax.axis_index("expert")
     t = lax.axis_index("tensor")
     me = e * SHARES + t
-
-    barrier = pltpu.get_barrier_semaphore()
-
-    def greet(k, _):
-        p = lax.rem(me + k, OWNERS)
-        pl.semaphore_signal(barrier, inc=1, device_id=(p // SHARES, lax.rem(p, SHARES)), device_id_type=MESH)
-        return 0
+    x, y, core = lax.div(e, 4), lax.rem(t, 4), lax.rem(e, 2)
+    high, low = lax.div(t, 4), lax.rem(lax.div(e, 2), 2)
+    z = high * 2 + low
+
+    def step(v, d):
+        return lax.rem(v + d, 4)
+
+    def at(x, y, z, core):
+        return x * 4 + lax.rem(z, 2) * 2 + core, lax.div(z, 2) * 4 + y
 
     load_delta = pltpu.make_async_copy(delta.at[0], held, load_sem.at[0])
     load_delta.start()
-    lax.fori_loop(1, OWNERS, greet, 0)
-    own_rows = pltpu.make_async_copy(
-        attn_delta.at[:, pl.ds(pl.multiple_of(t * ATT_COLS, ATT_COLS), ATT_COLS)], gath.at[me], load_sem.at[1]
-    )
-    own_rows.start()
+
+    barrier = pltpu.get_barrier_semaphore()
+    for de in range(EXPERTS):
+        for dt in range(SHARES):
+            if de or dt:
+                pl.semaphore_signal(
+                    barrier, inc=1, device_id=(lax.rem(e + de, EXPERTS), lax.rem(t + dt, SHARES)), device_id_type=MESH
+                )
+
+    def columns(there, y):
+        share = lax.div(there, 2) * 4 + y
+        return attn_delta.at[:, pl.ds(pl.multiple_of(share * ATT_COLS, BLK), ATT_COLS)]
+
+    mine = z * 4 + y
+    own = pltpu.make_async_copy(columns(z, y), gath.at[core, x, mine], load_sem.at[1])
+    own.start()
     load_att = pltpu.make_async_copy(attn_shadow, att_old, load_sem.at[2])
     load_att.start()
     load_exp = pltpu.make_async_copy(expert_shadow.at[0], shadow, load_sem.at[3])
@@ -80,19 +89,18 @@
 
     pl.semaphore_wait(barrier, OWNERS - 1)
 
-    for k in range(1, SHARES):
-        q = lax.rem(t + k, SHARES)
+    for k in (10, 5, 15, 7, 13, 2, 8, 9, 6, 11, 14, 1, 4, 3, 12):
+        there, over = step(z, k // 4), step(y, k % 4)
         pltpu.make_async_remote_copy(
-            src_ref=attn_delta.at[:, pl.ds(pl.multiple_of(q * ATT_COLS, ATT_COLS), ATT_COLS)],
-            dst_ref=gath.at[me],
-            send_sem=a_send,
-            recv_sem=a_recv,
-            device_id=(e, q),
-            device_id_type=MESH,
+            src_ref=columns(there, over), dst_ref=gath.at[core, x, mine], send_sem=first_send, recv_sem=first_recv,
+            device_id=at(x, over, there, core), device_id_type=MESH,
         ).start()
 
     def send_block(k, _):
-        pe, pt = peer_at(e, t, k)
+        s = lax.rem(k * STRIDE, 32)
+        dx = jnp.where(k <= 32, 2, jnp.where(k <= 64, 1, jnp.where(k <= 96, 3, 0)))
+        dy, dz = lax.div(s, 8), lax.rem(lax.div(s, 2), 4)
+        pe, pt = at(step(x, dx), step(y, dy), step(z, dz), lax.rem(core + s, 2))
         p = pe * SHARES + pt
         send[p] = block_of(pe, pt)
         pltpu.make_async_remote_copy(
@@ -105,44 +113,57 @@
         ).start()
         return 0
 
-    lax.fori_loop(1, 33, send_block, 0)
-
-    own_rows.wait()
-    pltpu.make_async_copy(gath.at[pl.ds(0, 7)], gath.at[pl.ds(0, 7)], a_recv).wait()
-
-    core = lax.rem(e, 2)
-
-    def chunk(i):
-        return gath.at[pl.ds(pl.multiple_of(i * SHARES, SHARES), SHARES)]
-
-    def to_chip(h):
+    lax.fori_loop(1, AHEAD, send_block, 0)
+
+    own.wait()
+    landed = gath.at[0, 0, pl.ds(0, 15)]
+    pltpu.make_async_copy(landed, landed, first_recv).wait()
+
+    sides = (1, 3)
+
+    def half(h):
+        return pl.ds(8 * h, 8)
+
+    def hand(i, rows, to, sent, got):
+        ref = gath.at[core, i, rows]
         return pltpu.make_async_remote_copy(
-            src_ref=chunk(e), dst_ref=chunk(e), send_sem=b_send.at[h], recv_sem=b_recv.at[h],
-            device_id=(lax.rem(e + 2 * h, EXPERTS), t), device_id_type=MESH,
+            src_ref=ref, dst_ref=ref, send_sem=sent, recv_sem=got, device_id=to, device_id_type=MESH
         )
 
-    def to_core(h):
-        src = lax.rem(e + EXPERTS - 2 * h, EXPERTS)
-        return pltpu.make_async_remote_copy(
-            src_ref=chunk(src), dst_ref=chunk(src), send_sem=c_send.at[h], recv_sem=c_recv.at[h],
-            device_id=(e + 1 - 2 * core, t), device_id_type=MESH,
+    def beside(n, h):
+        return hand(x, half(h), at(step(x, sides[n]), y, z, core), second_send.at[n, h], second_recv.at[n, h])
+
+    def onward(n):
+        return hand(
+            step(x, 4 - sides[n]), half(n), at(step(x, sides[n]), y, z, core), third_send.at[n], third_recv.at[n]
         )
 
-    to_core(0).start()
-    for h in range(1, 8):
-        to_chip(h).start()
-
-    lax.fori_loop(33, OWNERS, send_block, 0)
-
-    for h in range(1, 8):
-        to_chip(h).wait_recv()
-        to_core(h).start()
-    for h in range(8):
-        to_core(h).wait_recv()
-
-    load_att.wait()
-    for i in range(OWNERS):
-        att_wide[i // 2, (i % 2) * 4:(i % 2) * 4 + 4, :] = gath[i].astype(F32)
+    def across(n):
+        i, rows = ((0, pl.ds(0, 16)), (3, pl.ds(0, 16)), (1, pl.ds(0, 16)), (2, half(0)), (2, half(1)))[n]
+        return hand(step(x, i), rows, at(x, y, z, 1 - core), last_send.at[n], last_recv.at[n])
+
+    k = AHEAD
+    for start in (
+        beside(0, 0).start, beside(1, 1).start, beside(0, 1).start, beside(1, 0).start, across(0).start
+    ):
+        start()
+        lax.fori_loop(k, k + BETWEEN, send_block, 0)
+        k += BETWEEN
+    lax.fori_loop(k, UPTO, send_block, 0)
+    for n in range(2):
+        beside(n, n).wait_recv()
+        onward(n).start()
+    lax.fori_loop(UPTO, OWNERS, send_block, 0)
+
+    def att_widen(m, _):
+        i, j = lax.div(m, 4), lax.rem(m, 4)
+        gx, gc = lax.div(i, 4), lax.rem(i, 2)
+        gz = lax.div(j, 2) * 2 + lax.rem(lax.div(i, 2), 2)
+        for n in range(2):
+            owner = gz * 4 + lax.rem(j, 2) * 2 + n
+            rows = slice(4 * n, 4 * n + 4)
+            att_wide[m, rows, :] = gath[gc, gx, owner].astype(F32)
+        return 0
 
     def att_tile_row(i, _):
         tops = []
@@ -162,14 +183,36 @@
         attn_amax[pl.ds(i, 1), :] = row
         return 0
 
-    lax.fori_loop(0, 4, att_tile_row, 0)
+    load_att.wait()
+
+    def work(r):
+        i = step(x, r)
+        lax.fori_loop(i * 16, i * 16 + 16, att_widen, 0)
+        att_tile_row(i, 0)
+
+    across(0).wait_recv()
+    work(0)
+    for n in range(2):
+        beside(n, 1 - n).wait_recv()
+        across(1 + n).start()
+    for n in range(2):
+        across(1 + n).wait_recv()
+        work((3, 1)[n])
+    for n in range(2):
+        onward(n).wait_recv()
+        across(3 + n).start()
+    for n in range(2):
+        across(3 + n).wait_recv()
+    work(2)
 
     load_exp.wait()
-    pltpu.make_async_copy(gath.at[pl.ds(0, 7)], gath.at[pl.ds(0, 7)], a_send).wait()
-    for h in range(1, 8):
-        to_chip(h).wait_send()
-    for h in range(8):
-        to_core(h).wait_send()
+    pltpu.make_async_copy(landed, landed, first_send).wait()
+    for n in range(2):
+        beside(n, 0).wait_send()
+        beside(n, 1).wait_send()
+        onward(n).wait_send()
+    for n in range(5):
+        across(n).wait_send()
     whole = pl.ds(0, OWNERS - 1)
     pltpu.make_async_copy(send.at[whole], send.at[whole], send_sem).wait()
     pltpu.make_async_copy(recv.at[whole], recv.at[whole], recv_sem).wait()
@@ -182,6 +225,9 @@
 ):
     copy_an = pltpu.make_async_copy(att_new_v, attn_new, out_sem.at[0])
     copy_ac = pltpu.make_async_copy(att_codes_v, attn_codes, out_sem.at[1])
+
+    copy_an.start()
+    copy_ac.start()
 
     def invert(l, _):
         place[owner[l]] = l
@@ -215,8 +261,6 @@
         copy_codes(s).start()
         return 0
 
-    copy_an.start()
-    copy_ac.start()
     lax.fori_loop(0, SUPER, group, 0)
     att_small[...] = att_amax_v[:, :ATT_TILES]
     copy_am = pltpu.make_async_copy(amax_v, expert_amax.at[0], out_sem.at[2])
@@ -237,15 +281,16 @@
     smem = pl.BlockSpec(memory_space=pltpu.SMEM)
     dma = pltpu.SemaphoreType.DMA
     shape = jax.ShapeDtypeStruct
+    in_hbm = functools.partial(pltpu.with_memory_space_constraint, memory_space=pltpu.HBM)
     recv, shadow, att_new_v, att_codes_v, att_amax_v = pl.pallas_call(
         exchange,
         name="exchange",
         out_shape=(
-            shape((OWNERS, RB, BLK), BF16),
-            shape((ROWS, BLK), F32),
-            shape((64, 8, ATT_COLS), F32),
-            shape((512, ATT_COLS), BF16),
-            shape((4, BLK), F32),
+            pltpu.VMEM((OWNERS, RB, BLK), BF16),
+            pltpu.VMEM((ROWS, BLK), F32),
+            pltpu.VMEM((64, 8, ATT_COLS), F32),
+            pltpu.VMEM((512, ATT_COLS), BF16),
+            pltpu.VMEM((4, BLK), F32),
         ),
         in_specs=[hbm] * 4,
         out_specs=(vmem,) * 5,
@@ -253,16 +298,16 @@
             pltpu.VMEM((RB, EXPERTS, 1024), BF16),
             pltpu.VMEM((SHARES, RB * EXPERTS, BLK), F32),
             pltpu.VMEM((OWNERS, RB, BLK), BF16),
-            pltpu.VMEM((OWNERS, ATT_ROWS, ATT_COLS), BF16),
+            pltpu.VMEM((2, 4, 16, ATT_ROWS, ATT_COLS), BF16),
             pltpu.VMEM((64, 8, ATT_COLS), F32),
             pltpu.VMEM((64, 8, ATT_COLS), F32),
             dma((4,)), dma(()), dma(()), dma(()), dma(()),
-            dma((8,)), dma((8,)), dma((8,)), dma((8,)),
+            dma((2, 2)), dma((2, 2)), dma((2,)), dma((2,)), dma((5,)), dma((5,)),
         ],
         compiler_params=pltpu.CompilerParams(
             collective_id=0, has_side_effects=True, vmem_limit_bytes=40 << 20
         ),
-    )(learner_delta, attn_delta, attn_shadow.reshape(64, 8, ATT_COLS), expert_shadow)
+    )(*(in_hbm(x) for x in (learner_delta, attn_delta, attn_shadow.reshape(64, 8, ATT_COLS), expert_shadow)))
 
     return pl.pallas_call(
         finish,

time: 64.1 us -> 49.3 us (0.77)
  Pallas kernels: 56.2 us -> 48.5 us
  local copies, waits for them, and re-layouts: 6.62 us -> 0.01 us
    pallas_call x1, Pallas kernels: 51.1 us -> 43.6 us  [on_device(): pl.pallas_call(exchange, name='exchange', out_shape=(pltpu.VMEM((OWNERS,...]
    unnamed x12 -> x4, local copies, waits for them, and re-layouts: 6.62 us -> 0.01 us
where the time goes in v3:
time: 49.3 us; the launch traced here: 49.2 us
  Pallas kernels  48.5 us (98%)
  between operations  0.67 us (1%)
    pallas_call x1, Pallas kernels, on_device(): pl.pallas_call(exchange, name='exchange', out_shape=(pltpu.VMEM((OWNERS,...  43.6 us
    pallas_call x1, Pallas kernels, on_device(): pl.pallas_call(finish, name='finish', out_shape=(shape((1, ROWS, BLK), F3...  4.89 us

profile of v3, /device:TPU:1, one launch (start us, length us, event | category | flops | bytes accessed | tf_op | source)
XLA Modules:
  0.0 49.2 jit_solution(2380576119146460145)
XLA Ops:
  0.6 0.0 copy-start
  0.6 0.0 copy-start.1
  0.7 43.6 %exchange.1 = (bf16[128,56,128]{2,1,0:T(8,128)(2,1)S(1)}, f32[7168,128]{1,0:T(8,128)S(1)}, f32[64,8,2048]{2,1,0:T(8,128)S(1)}, bf16[512,2048]{1,0:T(8,128)(2,1)S(1)}, f32[4,128]{1,0:T(4,128)S(1)}) custom-call(bf16[1,56,16,1024]{3,2,1,0:T(8,128)(2,1)} %delta.1, bf16[4,16384]{1,0:T(4,128)(2,1)} %attn_delta.1, f32[64,8,2048]{2,1,0:T(8,128)} %bitcast.5, ...), custom_call_target="tpu_custom_call" | custom-call | tf_op jit(solution)/shard_map/exchange/pallas_call | solution.py:285
  44.3 0.0 copy-done
  44.3 0.0 copy-done.1
  44.3 4.9 %finish.1 = (f32[1,7168,128]{2,1,0:T(8,128)}, bf16[1,7168,128]{2,1,0:T(8,128)(2,1)}, f32[1,56,128]{2,1,0:T(8,128)}, f32[512,2048]{1,0:T(8,128)}, bf16[512,2048]{1,0:T(8,128)(2,1)}, /*index=5*/f32[4,16]{1,0:T(4,128)}) custom-call(s32[128]{0:T(128)S(1)} %copy-done, s32[56]{0:T(128)S(1)} %bitcast.4, bf16[128,56,128]{2,1,0:T(8,128)(2,1)S(1)} %get-tuple-element.11.recv, ...), custom_call_target="tpu_custom_call" | custom-call | tf_op jit(solution)/shard_map/finish/pallas_call | solution.py:312
Async XLA Ops:
  0.6 43.7 %copy-start = (s32[128]{0:T(128)S(1)}, s32[128]{0:T(128)}, u32[]{:S(2)}) copy-start(s32[128]{0:T(128)} %owner.1) | copy-start | bytes 1540
  0.6 43.7 %copy-start.1 = (s32[1,56,1]{1,2,0:T(1,128)S(1)}, s32[1,56,1]{1,2,0:T(1,128)}, u32[]{:S(2)}) copy-start(s32[1,56,1]{1,2,0:T(1,128)} %param.9) | copy-start | bytes 676

commit v4 on v3

--- a/solution.py
+++ b/solution.py
@@ -25,7 +25,7 @@
 TILES = 7
 
 
-AHEAD, BETWEEN, UPTO = 50, 4, 90
+AHEAD, BETWEEN, UPTO = 65, 4, 127
 STRIDE = 21
 
 
@@ -97,8 +97,9 @@
         ).start()
 
     def send_block(k, _):
-        s = lax.rem(k * STRIDE, 32)
-        dx = jnp.where(k <= 32, 2, jnp.where(k <= 64, 1, jnp.where(k <= 96, 3, 0)))
+        n = k - 1
+        s = lax.rem((n + 1) * STRIDE, 32)
+        dx = jnp.where(n < 32, 2, jnp.where(n < 64, 1, jnp.where(n < 96, 3, 0)))
         dy, dz = lax.div(s, 8), lax.rem(lax.div(s, 2), 4)
         pe, pt = at(step(x, dx), step(y, dy), step(z, dz), lax.rem(core + s, 2))
         p = pe * SHARES + pt
@@ -219,15 +220,24 @@
 
 
 def finish(
-    owner, mode, recv, shadow, att_new_v, att_codes_v, att_amax_v,
+    owner_v, mode_v, recv, shadow, att_new_v, att_codes_v, att_amax_v,
     expert_new, expert_codes, expert_amax, attn_new, attn_codes, attn_amax,
-    place, new_v, codes_v, amax_v, att_small, out_sem, new_sem, codes_sem,
+    owner, mode, place, new_v, codes_v, amax_v, att_small, out_sem, new_sem, codes_sem,
 ):
     copy_an = pltpu.make_async_copy(att_new_v, attn_new, out_sem.at[0])
     copy_ac = pltpu.make_async_copy(att_codes_v, attn_codes, out_sem.at[1])
 
+    copy_owner = pltpu.make_async_copy(owner_v, owner, out_sem.at[4])
+    copy_mode = pltpu.make_async_copy(mode_v, mode, out_sem.at[5])
+    copy_owner.start()
+    copy_mode.start()
     copy_an.start()
     copy_ac.start()
+    att_small[...] = att_amax_v[:, :ATT_TILES]
+    copy_aa = pltpu.make_async_copy(att_small, attn_amax, out_sem.at[3])
+    copy_aa.start()
+    copy_owner.wait()
+    copy_mode.wait()
 
     def invert(l, _):
         place[owner[l]] = l
@@ -262,11 +272,8 @@
         return 0
 
     lax.fori_loop(0, SUPER, group, 0)
-    att_small[...] = att_amax_v[:, :ATT_TILES]
     copy_am = pltpu.make_async_copy(amax_v, expert_amax.at[0], out_sem.at[2])
     copy_am.start()
-    copy_aa = pltpu.make_async_copy(att_small, attn_amax, out_sem.at[3])
-    copy_aa.start()
     copy_an.wait()
     copy_ac.wait()
     copy_am.wait()
@@ -278,7 +285,6 @@
 def on_device(learner_delta, owner_block, expert_shadow, tile_mode, attn_delta, attn_shadow):
     vmem = pl.BlockSpec(memory_space=pltpu.VMEM)
     hbm = pl.BlockSpec(memory_space=pltpu.HBM)
-    smem = pl.BlockSpec(memory_space=pltpu.SMEM)
     dma = pltpu.SemaphoreType.DMA
     shape = jax.ShapeDtypeStruct
     in_hbm = functools.partial(pltpu.with_memory_space_constraint, memory_space=pltpu.HBM)
@@ -320,15 +326,17 @@
             shape((512, ATT_COLS), BF16),
             shape((4, ATT_TILES), F32),
         ),
-        in_specs=[smem, smem] + [vmem] * 5,
+        in_specs=[vmem] * 7,
         out_specs=(hbm,) * 6,
         scratch_shapes=[
+            pltpu.SMEM((OWNERS,), jnp.int32),
+            pltpu.SMEM((ROWS // BLK,), jnp.int32),
             pltpu.SMEM((OWNERS,), jnp.int32),
             pltpu.VMEM((ROWS, BLK), F32),
             pltpu.VMEM((ROWS, BLK), BF16),
             pltpu.VMEM((ROWS // BLK, BLK), F32),
             pltpu.VMEM((4, ATT_TILES), F32),
-            dma((4,)), dma(()), dma(()),
+            dma((6,)), dma(()), dma(()),
         ],
         compiler_params=pltpu.CompilerParams(vmem_limit_bytes=40 << 20),
     )(owner_block, tile_mode.reshape(ROWS // BLK), recv, shadow, att_new_v.reshape(512, ATT_COLS), att_codes_v, att_amax_v)

time: 49.3 us -> 48.8 us (0.990)
  Pallas kernels: 48.5 us -> 48 us
    pallas_call x1, Pallas kernels: 4.89 us -> 4.37 us  [on_device(): pl.pallas_call(finish, name='finish', out_shape=(shape((1, ROWS, BLK), F3...]
where the time goes in v4:
time: 48.8 us; the launch traced here: 48.7 us
  Pallas kernels  48 us (98%)
  between operations  0.67 us (1%)
    pallas_call x1, Pallas kernels, on_device(): pl.pallas_call(exchange, name='exchange', out_shape=(pltpu.VMEM((OWNERS,...  43.6 us
    pallas_call x1, Pallas kernels, on_device(): pl.pallas_call(finish, name='finish', out_shape=(shape((1, ROWS, BLK), F3...  4.37 us

profile of v4, /device:TPU:1, one launch (start us, length us, event | category | flops | bytes accessed | tf_op | source)
XLA Modules:
  0.0 48.7 jit_solution(2389511199701051369)
XLA Ops:
  0.6 0.0 copy-start
  0.6 0.0 copy-start.1
  0.7 43.6 %exchange.1 = (bf16[128,56,128]{2,1,0:T(8,128)(2,1)S(1)}, f32[7168,128]{1,0:T(8,128)S(1)}, f32[64,8,2048]{2,1,0:T(8,128)S(1)}, bf16[512,2048]{1,0:T(8,128)(2,1)S(1)}, f32[4,128]{1,0:T(4,128)S(1)}) custom-call(bf16[1,56,16,1024]{3,2,1,0:T(8,128)(2,1)} %delta.1, bf16[4,16384]{1,0:T(4,128)(2,1)} %attn_delta.1, f32[64,8,2048]{2,1,0:T(8,128)} %bitcast.5, ...), custom_call_target="tpu_custom_call" | custom-call | tf_op jit(solution)/shard_map/exchange/pallas_call | solution.py:291
  44.3 0.0 copy-done
  44.3 0.0 copy-done.1
  44.3 4.4 %finish.1 = (f32[1,7168,128]{2,1,0:T(8,128)}, bf16[1,7168,128]{2,1,0:T(8,128)(2,1)}, f32[1,56,128]{2,1,0:T(8,128)}, f32[512,2048]{1,0:T(8,128)}, bf16[512,2048]{1,0:T(8,128)(2,1)}, /*index=5*/f32[4,16]{1,0:T(4,128)}) custom-call(s32[128]{0:T(128)S(1)} %copy-done, s32[56]{0:T(128)S(1)} %bitcast.4, bf16[128,56,128]{2,1,0:T(8,128)(2,1)S(1)} %get-tuple-element.11.recv, ...), custom_call_target="tpu_custom_call" | custom-call | tf_op jit(solution)/shard_map/finish/pallas_call | solution.py:318
Async XLA Ops:
  0.6 43.7 %copy-start = (s32[128]{0:T(128)S(1)}, s32[128]{0:T(128)}, u32[]{:S(2)}) copy-start(s32[128]{0:T(128)} %owner_v.1) | copy-start | bytes 1540
  0.6 43.7 %copy-start.1 = (s32[1,56,1]{1,2,0:T(1,128)S(1)}, s32[1,56,1]{1,2,0:T(1,128)}, u32[]{:S(2)}) copy-start(s32[1,56,1]{1,2,0:T(1,128)} %param.9) | copy-start | bytes 676

commit v5 on v4

--- a/solution.py
+++ b/solution.py
@@ -52,13 +52,16 @@
     load_delta = pltpu.make_async_copy(delta.at[0], held, load_sem.at[0])
     load_delta.start()
 
+    to_x = [step(x, d) * 4 for d in range(4)]
+    to_y = [step(y, d) for d in range(4)]
+    to_z = [(lax.rem(step(z, d), 2) * 2, lax.div(step(z, d), 2) * 4) for d in range(4)]
+    to_core = (core, 1 - core)
     barrier = pltpu.get_barrier_semaphore()
-    for de in range(EXPERTS):
-        for dt in range(SHARES):
-            if de or dt:
-                pl.semaphore_signal(
-                    barrier, inc=1, device_id=(lax.rem(e + de, EXPERTS), lax.rem(t + dt, SHARES)), device_id_type=MESH
-                )
+    for s in sorted(range(1, OWNERS), key=lambda s: -sum(min(d, 4 - d) for d in (s // 32, s // 8 % 4, s // 2 % 4))):
+        near, far = to_z[s // 2 % 4]
+        pl.semaphore_signal(
+            barrier, inc=1, device_id=(to_x[s // 32] + near + to_core[s % 2], far + to_y[s // 8 % 4]), device_id_type=MESH
+        )
 
     def columns(there, y):
         share = lax.div(there, 2) * 4 + y
@@ -97,9 +100,8 @@
         ).start()
 
     def send_block(k, _):
-        n = k - 1
-        s = lax.rem((n + 1) * STRIDE, 32)
-        dx = jnp.where(n < 32, 2, jnp.where(n < 64, 1, jnp.where(n < 96, 3, 0)))
+        s = lax.rem(k * STRIDE, 32)
+        dx = jnp.where(k <= 32, 2, jnp.where(k <= 64, 1, jnp.where(k <= 96, 3, 0)))
         dy, dz = lax.div(s, 8), lax.rem(lax.div(s, 2), 4)
         pe, pt = at(step(x, dx), step(y, dy), step(z, dz), lax.rem(core + s, 2))
         p = pe * SHARES + pt
@@ -302,7 +304,7 @@
         out_specs=(vmem,) * 5,
         scratch_shapes=[
             pltpu.VMEM((RB, EXPERTS, 1024), BF16),
-            pltpu.VMEM((SHARES, RB * EXPERTS, BLK), F32),
+            pltpu.VMEM((SHARES, RB * EXPERTS + EXPERTS, BLK), F32),
             pltpu.VMEM((OWNERS, RB, BLK), BF16),
             pltpu.VMEM((2, 4, 16, ATT_ROWS, ATT_COLS), BF16),
             pltpu.VMEM((64, 8, ATT_COLS), F32),

time: 48.8 us -> 48.7 us (level)
  no operation moved by 1% of the time
where the time goes in v5:
time: 48.7 us; the launch traced here: 48.6 us
  Pallas kernels  47.9 us (98%)
  between operations  0.67 us (1%)
    pallas_call x1, Pallas kernels, on_device(): pl.pallas_call(exchange, name='exchange', out_shape=(pltpu.VMEM((OWNERS,...  43.6 us
    pallas_call x1, Pallas kernels, on_device(): pl.pallas_call(finish, name='finish', out_shape=(shape((1, ROWS, BLK), F3...  4.37 us

profile of v5, /device:TPU:1, one launch (start us, length us, event | category | flops | bytes accessed | tf_op | source)
XLA Modules:
  0.0 48.6 jit_solution(10520838900955723369)
XLA Ops:
  0.6 0.0 copy-start
  0.6 0.0 copy-start.1
  0.7 43.6 %exchange.1 = (bf16[128,56,128]{2,1,0:T(8,128)(2,1)S(1)}, f32[7168,128]{1,0:T(8,128)S(1)}, f32[64,8,2048]{2,1,0:T(8,128)S(1)}, bf16[512,2048]{1,0:T(8,128)(2,1)S(1)}, f32[4,128]{1,0:T(4,128)S(1)}) custom-call(bf16[1,56,16,1024]{3,2,1,0:T(8,128)(2,1)} %delta.1, bf16[4,16384]{1,0:T(4,128)(2,1)} %attn_delta.1, f32[64,8,2048]{2,1,0:T(8,128)} %bitcast.5, ...), custom_call_target="tpu_custom_call" | custom-call | tf_op jit(solution)/shard_map/exchange/pallas_call | solution.py:293
  44.2 0.0 copy-done
  44.2 0.0 copy-done.1
  44.2 4.4 %finish.1 = (f32[1,7168,128]{2,1,0:T(8,128)}, bf16[1,7168,128]{2,1,0:T(8,128)(2,1)}, f32[1,56,128]{2,1,0:T(8,128)}, f32[512,2048]{1,0:T(8,128)}, bf16[512,2048]{1,0:T(8,128)(2,1)}, /*index=5*/f32[4,16]{1,0:T(4,128)}) custom-call(s32[128]{0:T(128)S(1)} %copy-done, s32[56]{0:T(128)S(1)} %bitcast.4, bf16[128,56,128]{2,1,0:T(8,128)(2,1)S(1)} %get-tuple-element.11.recv, ...), custom_call_target="tpu_custom_call" | custom-call | tf_op jit(solution)/shard_map/finish/pallas_call | solution.py:320
Async XLA Ops:
  0.6 43.6 %copy-start = (s32[128]{0:T(128)S(1)}, s32[128]{0:T(128)}, u32[]{:S(2)}) copy-start(s32[128]{0:T(128)} %owner_v.1) | copy-start | bytes 1540
  0.6 43.6 %copy-start.1 = (s32[1,56,1]{1,2,0:T(1,128)S(1)}, s32[1,56,1]{1,2,0:T(1,128)}, u32[]{:S(2)}) copy-start(s32[1,56,1]{1,2,0:T(1,128)} %param.9) | copy-start | bytes 676

commit v6 on v5

--- a/solution.py
+++ b/solution.py
@@ -25,7 +25,7 @@
 TILES = 7
 
 
-AHEAD, BETWEEN, UPTO = 65, 4, 127
+AHEAD, BETWEEN, UPTO = 45, 0, 127
 STRIDE = 21
 
 

time: 48.7 us -> 48.7 us (level)
  no operation moved by 1% of the time
where the time goes in v6:
time: 48.7 us; the launch traced here: 48.6 us
  Pallas kernels  47.9 us (98%)
  between operations  0.67 us (1%)
    pallas_call x1, Pallas kernels, on_device(): pl.pallas_call(exchange, name='exchange', out_shape=(pltpu.VMEM((OWNERS,...  43.6 us
    pallas_call x1, Pallas kernels, on_device(): pl.pallas_call(finish, name='finish', out_shape=(shape((1, ROWS, BLK), F3...  4.37 us

profile of v6, /device:TPU:1, one launch (start us, length us, event | category | flops | bytes accessed | tf_op | source)
XLA Modules:
  0.0 48.6 jit_solution(18240907074247597318)
XLA Ops:
  0.6 0.0 copy-start
  0.6 0.0 copy-start.1
  0.7 43.6 %exchange.1 = (bf16[128,56,128]{2,1,0:T(8,128)(2,1)S(1)}, f32[7168,128]{1,0:T(8,128)S(1)}, f32[64,8,2048]{2,1,0:T(8,128)S(1)}, bf16[512,2048]{1,0:T(8,128)(2,1)S(1)}, f32[4,128]{1,0:T(4,128)S(1)}) custom-call(bf16[1,56,16,1024]{3,2,1,0:T(8,128)(2,1)} %delta.1, bf16[4,16384]{1,0:T(4,128)(2,1)} %attn_delta.1, f32[64,8,2048]{2,1,0:T(8,128)} %bitcast.5, ...), custom_call_target="tpu_custom_call" | custom-call | tf_op jit(solution)/shard_map/exchange/pallas_call | solution.py:293
  44.2 0.0 copy-done
  44.2 0.0 copy-done.1
  44.2 4.4 %finish.1 = (f32[1,7168,128]{2,1,0:T(8,128)}, bf16[1,7168,128]{2,1,0:T(8,128)(2,1)}, f32[1,56,128]{2,1,0:T(8,128)}, f32[512,2048]{1,0:T(8,128)}, bf16[512,2048]{1,0:T(8,128)(2,1)}, /*index=5*/f32[4,16]{1,0:T(4,128)}) custom-call(s32[128]{0:T(128)S(1)} %copy-done, s32[56]{0:T(128)S(1)} %bitcast.4, bf16[128,56,128]{2,1,0:T(8,128)(2,1)S(1)} %get-tuple-element.11.recv, ...), custom_call_target="tpu_custom_call" | custom-call | tf_op jit(solution)/shard_map/finish/pallas_call | solution.py:320
Async XLA Ops:
  0.6 43.6 %copy-start = (s32[128]{0:T(128)S(1)}, s32[128]{0:T(128)}, u32[]{:S(2)}) copy-start(s32[128]{0:T(128)} %owner_v.1) | copy-start | bytes 1540
  0.6 43.6 %copy-start.1 = (s32[1,56,1]{1,2,0:T(1,128)S(1)}, s32[1,56,1]{1,2,0:T(1,128)}, u32[]{:S(2)}) copy-start(s32[1,56,1]{1,2,0:T(1,128)} %param.9) | copy-start | bytes 676

commit v7 on v6

--- a/solution.py
+++ b/solution.py
@@ -25,7 +25,7 @@
 TILES = 7
 
 
-AHEAD, BETWEEN, UPTO = 45, 0, 127
+AHEAD, LATER, BETWEEN = 30, 65, 2
 STRIDE = 21
 
 
@@ -92,10 +92,10 @@
 
     pl.semaphore_wait(barrier, OWNERS - 1)
 
-    for k in (10, 5, 15, 7, 13, 2, 8, 9, 6, 11, 14, 1, 4, 3, 12):
+    for k in (2, 5, 7, 6, 1, 4, 3, 10, 15, 13, 8, 9, 11, 14, 12):
         there, over = step(z, k // 4), step(y, k % 4)
         pltpu.make_async_remote_copy(
-            src_ref=columns(there, over), dst_ref=gath.at[core, x, mine], send_sem=first_send, recv_sem=first_recv,
+            src_ref=columns(there, over), dst_ref=gath.at[core, x, mine], send_sem=first_send.at[k // 8], recv_sem=first_recv.at[k // 8],
             device_id=at(x, over, there, core), device_id_type=MESH,
         ).start()
 
@@ -119,13 +119,13 @@
     lax.fori_loop(1, AHEAD, send_block, 0)
 
     own.wait()
-    landed = gath.at[0, 0, pl.ds(0, 15)]
-    pltpu.make_async_copy(landed, landed, first_recv).wait()
+    landed = (gath.at[0, 0, pl.ds(0, 7)], gath.at[0, 0, pl.ds(0, 8)])
+    pltpu.make_async_copy(landed[0], landed[0], first_recv.at[0]).wait()
 
     sides = (1, 3)
 
-    def half(h):
-        return pl.ds(8 * h, 8)
+    def quarter(q):
+        return pl.ds(step(z, 4 - q) * 4, 4)
 
     def hand(i, rows, to, sent, got):
         ref = gath.at[core, i, rows]
@@ -133,30 +133,35 @@
             src_ref=ref, dst_ref=ref, send_sem=sent, recv_sem=got, device_id=to, device_id_type=MESH
         )
 
-    def beside(n, h):
-        return hand(x, half(h), at(step(x, sides[n]), y, z, core), second_send.at[n, h], second_recv.at[n, h])
-
-    def onward(n):
-        return hand(
-            step(x, 4 - sides[n]), half(n), at(step(x, sides[n]), y, z, core), third_send.at[n], third_recv.at[n]
-        )
+    def beside(n, q):
+        to = at(step(x, sides[n]), y, z, core)
+        return hand(x, quarter(q), to, second_send.at[n, q], second_recv.at[n, q])
+
+    def onward(n, q):
+        to = at(step(x, sides[n]), y, z, core)
+        return hand(step(x, 4 - sides[n]), quarter(q), to, third_send.at[q], third_recv.at[q])
 
     def across(n):
-        i, rows = ((0, pl.ds(0, 16)), (3, pl.ds(0, 16)), (1, pl.ds(0, 16)), (2, half(0)), (2, half(1)))[n]
-        return hand(step(x, i), rows, at(x, y, z, 1 - core), last_send.at[n], last_recv.at[n])
+        return hand(step(x, (0, 3, 1, 2)[n]), pl.ds(0, 16), at(x, y, z, 1 - core), last_send.at[n], last_recv.at[n])
 
     k = AHEAD
-    for start in (
-        beside(0, 0).start, beside(1, 1).start, beside(0, 1).start, beside(1, 0).start, across(0).start
-    ):
-        start()
+    for n, q in ((0, 0), (1, 1), (0, 1), (1, 0)):
+        beside(n, q).start()
         lax.fori_loop(k, k + BETWEEN, send_block, 0)
         k += BETWEEN
-    lax.fori_loop(k, UPTO, send_block, 0)
-    for n in range(2):
-        beside(n, n).wait_recv()
-        onward(n).start()
-    lax.fori_loop(UPTO, OWNERS, send_block, 0)
+    lax.fori_loop(k, LATER, send_block, 0)
+    pltpu.make_async_copy(landed[1], landed[1], first_recv.at[1]).wait()
+    k = LATER
+    for n, q in ((1, 2), (0, 3), (1, 3), (0, 2)):
+        beside(n, q).start()
+        lax.fori_loop(k, k + BETWEEN, send_block, 0)
+        k += BETWEEN
+    across(0).start()
+    lax.fori_loop(k, OWNERS - 1, send_block, 0)
+    for q in range(4):
+        beside(q // 2, q).wait_recv()
+        onward(q // 2, q).start()
+    lax.fori_loop(OWNERS - 1, OWNERS, send_block, 0)
 
     def att_widen(m, _):
         i, j = lax.div(m, 4), lax.rem(m, 4)
@@ -196,26 +201,26 @@
     across(0).wait_recv()
     work(0)
     for n in range(2):
-        beside(n, 1 - n).wait_recv()
+        for q in (2 - 2 * n, 3 - 2 * n):
+            beside(n, q).wait_recv()
         across(1 + n).start()
     for n in range(2):
         across(1 + n).wait_recv()
         work((3, 1)[n])
+    for q in range(4):
+        onward(q // 2, q).wait_recv()
+    across(3).start()
+    across(3).wait_recv()
+    work(2)
+
+    load_exp.wait()
     for n in range(2):
-        onward(n).wait_recv()
-        across(3 + n).start()
-    for n in range(2):
-        across(3 + n).wait_recv()
-    work(2)
-
-    load_exp.wait()
-    pltpu.make_async_copy(landed, landed, first_send).wait()
-    for n in range(2):
-        beside(n, 0).wait_send()
-        beside(n, 1).wait_send()
-        onward(n).wait_send()
-    for n in range(5):
-        across(n).wait_send()
+        pltpu.make_async_copy(landed[n], landed[n], first_send.at[n]).wait()
+        for q in range(4):
+            beside(n, q).wait_send()
+    for q in range(4):
+        onward(q // 2, q).wait_send()
+        across(q).wait_send()
     whole = pl.ds(0, OWNERS - 1)
     pltpu.make_async_copy(send.at[whole], send.at[whole], send_sem).wait()
     pltpu.make_async_copy(recv.at[whole], recv.at[whole], recv_sem).wait()
@@ -309,8 +314,8 @@
             pltpu.VMEM((2, 4, 16, ATT_ROWS, ATT_COLS), BF16),
             pltpu.VMEM((64, 8, ATT_COLS), F32),
             pltpu.VMEM((64, 8, ATT_COLS), F32),
-            dma((4,)), dma(()), dma(()), dma(()), dma(()),
-            dma((2, 2)), dma((2, 2)), dma((2,)), dma((2,)), dma((5,)), dma((5,)),
+            dma((4,)), dma(()), dma(()), dma((2,)), dma((2,)),
+            dma((2, 4)), dma((2, 4)), dma((4,)), dma((4,)), dma((4,)), dma((4,)),
         ],
         compiler_params=pltpu.CompilerParams(
             collective_id=0, has_side_effects=True, vmem_limit_bytes=40 << 20

time: 48.7 us -> 48.9 us (level)
  no operation moved by 1% of the time
where the time goes in v7:
time: 48.9 us; the launch traced here: 48.7 us
  Pallas kernels  48 us (98%)
  between operations  0.67 us (1%)
    pallas_call x1, Pallas kernels, on_device(): pl.pallas_call(exchange, name='exchange', out_shape=(pltpu.VMEM((OWNERS,...  43.7 us
    pallas_call x1, Pallas kernels, on_device(): pl.pallas_call(finish, name='finish', out_shape=(shape((1, ROWS, BLK), F3...  4.37 us

profile of v7, /device:TPU:1, one launch (start us, length us, event | category | flops | bytes accessed | tf_op | source)
XLA Modules:
  0.0 48.7 jit_solution(11537896395679968952)
XLA Ops:
  0.6 0.0 copy-start
  0.6 0.0 copy-start.1
  0.7 43.7 %exchange.1 = (bf16[128,56,128]{2,1,0:T(8,128)(2,1)S(1)}, f32[7168,128]{1,0:T(8,128)S(1)}, f32[64,8,2048]{2,1,0:T(8,128)S(1)}, bf16[512,2048]{1,0:T(8,128)(2,1)S(1)}, f32[4,128]{1,0:T(4,128)S(1)}) custom-call(bf16[1,56,16,1024]{3,2,1,0:T(8,128)(2,1)} %delta.1, bf16[4,16384]{1,0:T(4,128)(2,1)} %attn_delta.1, f32[64,8,2048]{2,1,0:T(8,128)} %bitcast.5, ...), custom_call_target="tpu_custom_call" | custom-call | tf_op jit(solution)/shard_map/exchange/pallas_call | solution.py:298
  44.3 0.0 copy-done
  44.3 0.0 copy-done.1
  44.4 4.4 %finish.1 = (f32[1,7168,128]{2,1,0:T(8,128)}, bf16[1,7168,128]{2,1,0:T(8,128)(2,1)}, f32[1,56,128]{2,1,0:T(8,128)}, f32[512,2048]{1,0:T(8,128)}, bf16[512,2048]{1,0:T(8,128)(2,1)}, /*index=5*/f32[4,16]{1,0:T(4,128)}) custom-call(s32[128]{0:T(128)S(1)} %copy-done, s32[56]{0:T(128)S(1)} %bitcast.4, bf16[128,56,128]{2,1,0:T(8,128)(2,1)S(1)} %get-tuple-element.11.recv, ...), custom_call_target="tpu_custom_call" | custom-call | tf_op jit(solution)/shard_map/finish/pallas_call | solution.py:325
Async XLA Ops:
  0.6 43.7 %copy-start = (s32[128]{0:T(128)S(1)}, s32[128]{0:T(128)}, u32[]{:S(2)}) copy-start(s32[128]{0:T(128)} %owner_v.1) | copy-start | bytes 1540
  0.6 43.7 %copy-start.1 = (s32[1,56,1]{1,2,0:T(1,128)S(1)}, s32[1,56,1]{1,2,0:T(1,128)}, u32[]{:S(2)}) copy-start(s32[1,56,1]{1,2,0:T(1,128)} %param.9) | copy-start | bytes 676
